TPU v7x, 256 devices: a whole 4x4x8 slice. The times are simulated.
256 devices in a mesh: pre: 8 (over z), req: 32 (over x, y, core).
Axes of the slice: x: 4, y: 4, z: 8, core: 2. Of those that a mesh axis runs over, the one named last changes fastest.
Arguments:
- queries: bfloat16 [32, 16384], P('req', 'pre'), may hold values from -120 to 120
- prefix_keys: bfloat16 [131072, 1024], P(('pre', 'req')), may hold values from -4.6 to 4.6
- prefix_values: bfloat16 [131072, 1024], P(('pre', 'req')), may hold values from -6 to 6
- suffix_keys: bfloat16 [32, 2048, 1024], P('req', 'pre'), may hold values from -8 to 8
- suffix_values: bfloat16 [32, 2048, 1024], P('req', 'pre'), may hold values from -6 to 6
- suffix_lengths: int32 [32], P('req'), may hold values from 1 to 2048, 32768 in all
Outputs:
- attention: bfloat16 [32, 16384], P('req', 'pre')
All inputs are finite; a program needn't handle non-finite values. No bound on the sum of `suffix_lengths` on one device may be relied on, other than what follows from the above.
Results may differ from a plain program's by a relative error of at most 0.0055.
Values may be sent and summed in bfloat16 or wider, within the bound.
A program may use at most 64 MiB of HBM per device.

v0:
```python
import functools
import math

import jax
import jax.numpy as jnp
from jax import lax
from jax.experimental import pallas as pl
from jax.experimental.pallas import tpu as pltpu
from jax.sharding import PartitionSpec as P

MESH = pl.DeviceIdType.MESH
DH = 128
HG = 16
F32 = jnp.float32
BF16 = jnp.bfloat16
SCALE = math.log2(math.e) / math.sqrt(DH)
NEG = -1e30


def plane_chips(nx, ny):
    def hops(o):
        return min(o[0], nx - o[0]) + min(o[1], ny - o[1])

    chips = sorted([(i, j) for i in range(nx) for j in range(ny)], key=lambda o: -hops(o))
    back = [chips.index(((-i) % nx, (-j) % ny)) for i, j in chips]
    return chips, back


def kernel(
    dims, row_chunks,
    q_ref, k_ref, v_ref, sk_ref, sv_ref, len_ref, out_ref,
    qrow, length, kb, vx, skb, svb, qy, qo, qa, ob, ib, st, ist, zo, zi, zst, zist, so, sst,
    local_sem, kvs_sem, kvr_sem, zs_sem, zr_sem, zd_sem, zo_sem, qs_sem, qr_sem, os_sem, or_sem, zz_sem, su_sem,
):
    npre, nx, ny = dims
    nreq = nx * ny * 2
    half = npre // 2
    tokens = k_ref.shape[0]
    slots = sk_ref.shape[1]
    p = lax.axis_index("pre")
    r = lax.axis_index("req")
    c = r % 2
    odd = 1 - c
    e = (p + odd) % 2
    x = r // (2 * ny)
    y = (r // 2) % ny
    chips, back = plane_chips(nx, ny)
    own_chip = len(chips) - 1

    def plane_mate(chip, core):
        kx, ky = chips[chip]
        return (((x + kx) % nx) * ny + (y + ky) % ny) * 2 + (c + core) % 2

    def pre_mate(k):
        return (p + k) % npre

    def columns(g):
        return pl.ds(pl.multiple_of(g * DH, DH), DH)

    def own_rows():
        return pl.ds(pl.multiple_of(c * tokens, tokens), tokens)

    def drain(ref, sem):
        pltpu.make_async_copy(ref, ref, sem).wait()

    barrier = pltpu.get_barrier_semaphore()
    sib = plane_mate(own_chip, 1)
    far_first = sorted(range(1, npre), key=lambda k: -min(k, npre - k))
    for mate in (r, sib):
        for k in far_first:
            pl.semaphore_signal(barrier, inc=1, device_id=(pre_mate(k), mate), device_id_type=MESH)
    for n in range(own_chip):
        pl.semaphore_signal(barrier, inc=1, device_id=(p, plane_mate(n, 0)), device_id_type=MESH)
    pl.semaphore_signal(barrier, inc=1, device_id=(p, sib), device_id_type=MESH)

    query_copy = pltpu.make_async_copy(q_ref, qrow, local_sem.at[4])
    query_copy.start()
    length_copy = pltpu.make_async_copy(len_ref, length, local_sem.at[5])
    length_copy.start()
    for i in range(half):
        pltpu.make_async_copy(k_ref.at[:, columns(2 * i + odd)], kb.at[i, own_rows(), :], local_sem.at[0]).start()
        pltpu.make_async_copy(
            v_ref.at[:, columns(2 * i + odd)], vx.at[i, own_rows(), pl.ds(0, DH)], local_sem.at[1]
        ).start()
    suffix = [
        pltpu.make_async_copy(sk_ref.at[0], skb, local_sem.at[2]),
        pltpu.make_async_copy(sv_ref.at[0], svb, local_sem.at[3]),
    ]
    for copy in suffix:
        copy.start()

    query_copy.wait()
    tile = jnp.concatenate([qrow[:, h * DH : (h + 1) * DH].astype(F32) for h in range(HG)], axis=0)
    tile = tile.astype(BF16)

    @pl.when(e == 0)
    def _():
        qy[p // 2, c] = tile

    @pl.when(e == 1)
    def _():
        qo[p // 2] = tile


    def fill(i, carry):
        vx[i, :, DH : 2 * DH] = jnp.ones((2 * tokens, DH), BF16)
        return carry

    lax.fori_loop(0, half, fill, 0)
    pl.semaphore_wait(barrier, 2 * (npre - 1) + own_chip + 1)

    def line_copy(src, dst, plane_index, mate, recv):
        return pltpu.make_async_remote_copy(
            src_ref=src, dst_ref=dst, send_sem=zs_sem.at[0], recv_sem=recv,
            device_id=(plane_index, mate), device_id_type=MESH,
        )

    @pl.when(e == 0)
    def _():
        for k in far_first:
            line_copy(qy.at[p // 2, c], qy.at[p // 2, c], pre_mate(k), r, zr_sem.at[p // 2]).start()

    @pl.when(e == 1)
    def _():
        for k in far_first + [0]:
            line_copy(qo.at[p // 2], qy.at[p // 2, c], pre_mate(k), sib, zd_sem.at[p // 2]).start()
        for k in far_first:
            line_copy(qo.at[p // 2], qo.at[p // 2], pre_mate(k), r, zo_sem.at[p // 2]).start()

    def forward(h):
        g = 2 * h + odd

        @pl.when(p != g)
        def _():
            drain(qy.at[h, c], zr_sem.at[h])

        drain(qy.at[h, 1 - c], zd_sem.at[h])
        for n in range(own_chip):
            pltpu.make_async_remote_copy(
                src_ref=qy.at[h], dst_ref=qa.at[back[n], h],
                send_sem=qs_sem.at[0], recv_sem=qr_sem.at[h],
                device_id=(p, plane_mate(n, 0)), device_id_type=MESH,
            ).start()
        qa[own_chip, h] = qy[h]

    for i in range(half):
        for n, (src, dst) in enumerate(
            (
                (k_ref.at[:, columns(2 * i + 1 - odd)], kb.at[i, own_rows(), :]),
                (v_ref.at[:, columns(2 * i + 1 - odd)], vx.at[i, own_rows(), pl.ds(0, DH)]),
            )
        ):
            pltpu.make_async_remote_copy(
                src_ref=src, dst_ref=dst, send_sem=kvs_sem.at[n], recv_sem=kvr_sem.at[n, i],
                device_id=(p, sib), device_id_type=MESH,
            ).start()

    def as_row(peak, total, lanes):
        count = peak.shape[0]
        at = lax.broadcasted_iota(jnp.int32, (count, DH), 1)
        row = lax.broadcasted_iota(jnp.int32, (count, DH), 0)
        return jnp.sum(jnp.where(at == row, peak, jnp.where(at == lanes + row, total, 0.0)), axis=0, keepdims=True)

    def weigh(rows, lanes):
        table = jnp.concatenate(rows, axis=0)
        top = jnp.max(table, axis=0, keepdims=True)
        factor = jnp.exp2(table - top)
        total = jnp.sum(factor * pltpu.roll(table, DH - lanes, 1), axis=0, keepdims=True)
        pad = jnp.zeros(((-len(rows) - 2) % 8, DH), F32)
        return jnp.concatenate([factor, top, total, pad], axis=0).T

    length_copy.wait()
    for copy in suffix:
        copy.wait()
    visible = (p * slots + lax.broadcasted_iota(jnp.int32, (HG, slots), 1)) < length[0]

    def suffix_part(g, q):
        span = columns(g)
        s = lax.dot_general(q, skb[:, span], (((1,), (1,)), ((), ())), preferred_element_type=F32)
        s = jnp.where(visible, s * SCALE, NEG)
        m = jnp.max(s, axis=1, keepdims=True)
        w = jnp.where(visible, jnp.exp2(s - m), 0.0).astype(BF16)
        so[g] = jnp.dot(w, svb[:, span], preferred_element_type=F32).astype(BF16)
        sst[g] = as_row(m, jnp.sum(w.astype(F32), axis=1, keepdims=True), HG)

    for h in range(half):
        forward(h)
    for h in range(half):

        @pl.when(p != 2 * h + 1 - odd)
        def _(h=h):
            drain(qo.at[h], zo_sem.at[h])

    for h in range(half):
        suffix_part(2 * h + odd, qy[h, c])
        suffix_part(2 * h + 1 - odd, qo[h])
    for k in far_first:
        g = pre_mate(k)
        for n, (src, dst) in enumerate(((so, zi), (sst, zist))):
            pltpu.make_async_remote_copy(
                src_ref=src.at[g], dst_ref=dst.at[npre + p], send_sem=su_sem.at[n], recv_sem=su_sem.at[2 + n],
                device_id=(g, r), device_id_type=MESH,
            ).start()
    zi[npre + p] = so[p]
    zist[npre + p] = sst[p]

    keys, values = kb.at[:, pl.ds(0, tokens), :], vx.at[:, pl.ds(0, tokens), pl.ds(0, DH)]
    drain(keys, local_sem.at[0])
    drain(values, local_sem.at[1])

    chunk = nreq // row_chunks
    per = chunk // 2
    pair_lane = lax.broadcasted_iota(jnp.int32, (chunk * HG, DH), 1)
    pair_row = lax.broadcasted_iota(jnp.int32, (chunk * HG, DH), 0) % (2 * HG)

    def group_step(i, carry):
        drain(kb.at[0, pl.ds(0, tokens)], kvr_sem.at[0, i])
        drain(vx.at[0, pl.ds(0, tokens), pl.ds(0, DH)], kvr_sem.at[1, i])
        drain(qa.at[pl.ds(0, own_chip), 0], qr_sem.at[i])

        def scores(ch):
            qc = qa[pl.ds(ch * per, per), i].reshape(chunk * HG, DH)
            return lax.dot_general(qc, kb[i], (((1,), (1,)), ((), ())), preferred_element_type=F32)

        s = scores(0)
        for ch in range(row_chunks):
            after = scores(ch + 1) if ch + 1 < row_chunks else None
            m = (jnp.max(s, axis=1, keepdims=True) * SCALE).astype(BF16).astype(F32)
            w = jnp.exp2(s * SCALE - m).astype(BF16)
            o = jnp.dot(w, vx[i], preferred_element_type=F32)
            ob[i, pl.ds(ch * per, per)] = o[:, :DH].astype(BF16).reshape(per, 2, HG, DH)
            stats = jnp.where(pair_lane == pair_row, m, 0.0)
            stats = jnp.where(pair_lane == DH // 2 + pair_row, o[:, DH:], stats)
            rows = jnp.sum(stats.reshape(per, 2 * HG, DH), axis=1)
            for n in range(per):
                st[i, ch * per + n] = rows[n : n + 1]
            s = after
        for n in range(own_chip):
            for a, (src, dst) in enumerate(((ob, ib), (st, ist))):
                pltpu.make_async_remote_copy(
                    src_ref=src.at[i, n], dst_ref=dst.at[i, back[n]],
                    send_sem=os_sem.at[a], recv_sem=or_sem.at[a, i],
                    device_id=(p, plane_mate(n, 0)), device_id_type=MESH,
                ).start()
        ib[i, own_chip] = ob[i, own_chip]
        ist[i, own_chip] = st[i, own_chip]
        return carry

    lax.fori_loop(0, half, group_step, 0)

    def combine_step(i, carry):
        drain(ist.at[i, pl.ds(0, own_chip)], or_sem.at[1, i])
        columns_of = weigh([ist[i, n] for n in range(len(chips))], DH // 2)[: 2 * HG]
        drain(ib.at[i, pl.ds(0, own_chip)], or_sem.at[0, i])
        num = functools.reduce(
            jnp.add,
            [columns_of[:, n : n + 1] * ib[i, n].reshape(2 * HG, DH).astype(F32) for n in range(len(chips))],
        )
        zo[i] = num.astype(BF16).reshape(2, HG, DH)
        for core in range(2):
            part = columns_of[HG * core : HG * (core + 1)]
            zst[i, core] = as_row(part[:, len(chips) : len(chips) + 1], part[:, len(chips) + 1 : len(chips) + 2], HG)
        g = 2 * i + odd

        def send(core, mate):
            for n, (src, dst) in enumerate(((zo, zi), (zst, zist))):
                pltpu.make_async_remote_copy(
                    src_ref=src.at[i, core], dst_ref=dst.at[p], send_sem=zz_sem.at[n], recv_sem=zz_sem.at[2 + n],
                    device_id=(g, mate), device_id_type=MESH,
                ).start()

        send(1 - c, sib)

        @pl.when(g != p)
        def _():
            send(c, r)

        @pl.when(g == p)
        def _():
            zi[p] = zo[i, c]
            zist[p] = zst[i, c]

        return carry

    lax.fori_loop(0, half, combine_step, 0)

    def both_cores(array, sem):
        @pl.when(e == 0)
        def _():
            drain(array.at[pl.ds(0, npre - 1)], sem)

        @pl.when(e == 1)
        def _():
            drain(array.at[pl.ds(0, npre)], sem)

    @pl.when(e == 0)
    def _():
        drain(zi.at[pl.ds(0, npre - 1)], zs_sem.at[0])

    @pl.when(e == 1)
    def _():
        drain(zi.at[pl.ds(0, 2 * npre - 1)], zs_sem.at[0])

    drain(keys, kvs_sem.at[0])
    drain(values, kvs_sem.at[1])
    drain(qa.at[pl.ds(0, own_chip)], qs_sem.at[0])
    drain(ib.at[:, pl.ds(0, own_chip)], os_sem.at[0])
    drain(ist.at[:, pl.ds(0, own_chip)], os_sem.at[1])
    drain(zi.at[pl.ds(0, npre - 1)], su_sem.at[0])
    drain(zist.at[pl.ds(0, npre - 1)], su_sem.at[1])
    drain(zi.at[pl.ds(0, npre - 1)], su_sem.at[2])
    drain(zist.at[pl.ds(0, npre - 1)], su_sem.at[3])
    both_cores(zist, zz_sem.at[3])
    columns_of = weigh([zist[k] for k in range(2 * npre)], HG)[:HG]
    both_cores(zi, zz_sem.at[2])
    num = functools.reduce(jnp.add, [columns_of[:, k : k + 1] * zi[k].astype(F32) for k in range(2 * npre)])
    result = (num / columns_of[:, 2 * npre + 1 : 2 * npre + 2]).astype(BF16)
    for h in range(HG):
        out_ref[:, h * DH : (h + 1) * DH] = result[h : h + 1]

    both_cores(zi, zz_sem.at[0])
    both_cores(zist, zz_sem.at[1])


def on_device(dims, row_chunks, queries, prefix_keys, prefix_values, suffix_keys, suffix_values, suffix_lengths):
    npre, nx, ny = dims
    nreq = nx * ny * 2
    half = npre // 2
    tokens = prefix_keys.shape[0]
    slots = suffix_keys.shape[1]
    width = npre * DH
    vmem = pl.BlockSpec(memory_space=pltpu.VMEM)
    hbm = pl.BlockSpec(memory_space=pl.ANY)
    dma = pltpu.SemaphoreType.DMA
    return pl.pallas_call(
        functools.partial(kernel, dims, row_chunks),
        out_shape=pltpu.VMEM((1, HG * DH), BF16),
        in_specs=[hbm] * 6,
        out_specs=vmem,
        scratch_shapes=[
            pltpu.VMEM((1, HG * DH), BF16),
            pltpu.SMEM((1,), jnp.int32),
            pltpu.VMEM((half, 2 * tokens, DH), BF16),
            pltpu.VMEM((half, 2 * tokens, 2 * DH), BF16),
            pltpu.VMEM((slots, width), BF16),
            pltpu.VMEM((slots, width), BF16),
            pltpu.VMEM((half, 2, HG, DH), BF16),
            pltpu.VMEM((half, HG, DH), BF16),
            pltpu.VMEM((nreq // 2, half, 2, HG, DH), BF16),
            pltpu.VMEM((half, nreq // 2, 2, HG, DH), BF16),
            pltpu.VMEM((half, nreq // 2, 2, HG, DH), BF16),
            pltpu.VMEM((half, nreq // 2, 1, DH), F32),
            pltpu.VMEM((half, nreq // 2, 1, DH), F32),
            pltpu.VMEM((half, 2, HG, DH), BF16),
            pltpu.VMEM((2 * npre, HG, DH), BF16),
            pltpu.VMEM((half, 2, 1, DH), F32),
            pltpu.VMEM((2 * npre, 1, DH), F32),
            pltpu.VMEM((npre, HG, DH), BF16),
            pltpu.VMEM((npre, 1, DH), F32),
            dma((6,)),
            dma((2,)),
            dma((2, half)),
            dma((1,)),
            dma((half,)),
            dma((half,)),
            dma((half,)),
            dma((1,)),
            dma((half,)),
            dma((2,)),
            dma((2, half)),
            dma((4,)),
            dma((4,)),
        ],
        compiler_params=pltpu.CompilerParams(
            collective_id=0, has_side_effects=True, vmem_limit_bytes=60 * 1024 * 1024
        ),
    )(queries, prefix_keys, prefix_values, suffix_keys, suffix_values, suffix_lengths)


def build(mesh, dims, row_chunks):
    placed = (
        P("req", "pre"),
        P(("pre", "req"), None),
        P(("pre", "req"), None),
        P("req", "pre", None),
        P("req", "pre", None),
        P("req"),
    )
    return jax.shard_map(
        functools.partial(on_device, dims, row_chunks),
        mesh=mesh, in_specs=placed, out_specs=P("req", "pre"), check_vma=False,
    )


def solution(mesh):
    return build(mesh, (8, 4, 4), 2)
```

profile of v0, /device:TPU:32, one launch (start us, length us, event | category | flops | bytes accessed | tf_op | source)
XLA Modules:
  0.0 31.4 jit_solution(14441424804149780404)
XLA Ops:
  0.7 30.2 %shard_map.64 = bf16[1,2048]{1,0:T(2,128)(2,1)S(1)} custom-call(bf16[1,2048]{1,0:T(2,128)(2,1)} %q_ref.1, bf16[512,1024]{1,0:T(8,128)(2,1)} %k_ref.1, bf16[512,1024]{1,0:T(8,128)(2,1)} %v_ref.1, bf16[1,256,1024]{2,1,0:T(8,128)(2,1)} %sk_ref.1, bf16[1,256,1024]{2,1,0:T(8,128)(2,1)} %sv_ref.1, s32[1]{0:T(128)S(6)} %copy.9.len_ref), custom_call_target="tpu_custom_call" | custom-call | tf_op jit(solution)/shard_map/pallas_call | solution.py:335
  30.8 0.6 %copy.8 = bf16[1,2048]{1,0:T(2,128)(2,1)} copy(bf16[1,2048]{1,0:T(2,128)(2,1)S(1)} %shard_map.64) | data formatting | bytes 8192
where the time goes:
time: 31.6 us; the launch traced here: 31.4 us
  Pallas kernels  30.2 us (96%)
  between operations  0.66 us (2%)
  local copies, waits for them, and re-layouts  0.6 us (2%)
    pallas_call x1, Pallas kernels, on_device(): pl.pallas_call(functools.partial(kernel, dims, row_chunks), out_shape=plt...  30.2 us

commit v1 on v0

--- a/solution.py
+++ b/solution.py
@@ -235,8 +235,8 @@
             for n in range(per):
                 st[i, ch * per + n] = rows[n : n + 1]
             s = after
-        for n in range(own_chip):
-            for a, (src, dst) in enumerate(((ob, ib), (st, ist))):
+        for a, (src, dst) in ((1, (st, ist)), (0, (ob, ib))):
+            for n in range(own_chip):
                 pltpu.make_async_remote_copy(
                     src_ref=src.at[i, n], dst_ref=dst.at[i, back[n]],
                     send_sem=os_sem.at[a], recv_sem=or_sem.at[a, i],
@@ -251,29 +251,30 @@
     def combine_step(i, carry):
         drain(ist.at[i, pl.ds(0, own_chip)], or_sem.at[1, i])
         columns_of = weigh([ist[i, n] for n in range(len(chips))], DH // 2)[: 2 * HG]
+        for core in range(2):
+            part = columns_of[HG * core : HG * (core + 1)]
+            zst[i, core] = as_row(part[:, len(chips) : len(chips) + 1], part[:, len(chips) + 1 : len(chips) + 2], HG)
+        g = 2 * i + odd
+
+        def send(src, dst, n):
+            for core, mate in ((c, r), (1 - c, sib)):
+                copy = pltpu.make_async_remote_copy(
+                    src_ref=src.at[i, core], dst_ref=dst.at[p], send_sem=zz_sem.at[n], recv_sem=zz_sem.at[2 + n],
+                    device_id=(g, mate), device_id_type=MESH,
+                )
+                if mate is sib:
+                    copy.start()
+                else:
+                    pl.when(g != p)(copy.start)
+
+        send(zst, zist, 1)
         drain(ib.at[i, pl.ds(0, own_chip)], or_sem.at[0, i])
         num = functools.reduce(
             jnp.add,
             [columns_of[:, n : n + 1] * ib[i, n].reshape(2 * HG, DH).astype(F32) for n in range(len(chips))],
         )
         zo[i] = num.astype(BF16).reshape(2, HG, DH)
-        for core in range(2):
-            part = columns_of[HG * core : HG * (core + 1)]
-            zst[i, core] = as_row(part[:, len(chips) : len(chips) + 1], part[:, len(chips) + 1 : len(chips) + 2], HG)
-        g = 2 * i + odd
-
-        def send(core, mate):
-            for n, (src, dst) in enumerate(((zo, zi), (zst, zist))):
-                pltpu.make_async_remote_copy(
-                    src_ref=src.at[i, core], dst_ref=dst.at[p], send_sem=zz_sem.at[n], recv_sem=zz_sem.at[2 + n],
-                    device_id=(g, mate), device_id_type=MESH,
-                ).start()
-
-        send(1 - c, sib)
-
-        @pl.when(g != p)
-        def _():
-            send(c, r)
+        send(zo, zi, 0)
 
         @pl.when(g == p)
         def _():

time: 31.6 us -> 31.4 us (level)
  Pallas kernels: 30.2 us -> 29.7 us
    pallas_call x1, Pallas kernels: 30.2 us -> 29.7 us  [on_device(): pl.pallas_call(functools.partial(kernel, dims, row_chunks), out_shape=plt...]
where the time goes in v1:
time: 31.4 us; the launch traced here: 31 us
  Pallas kernels  29.7 us (95%)
  between operations  0.66 us (2%)
  local copies, waits for them, and re-layouts  0.6 us (2%)
    pallas_call x1, Pallas kernels, on_device(): pl.pallas_call(functools.partial(kernel, dims, row_chunks), out_shape=plt...  29.7 us

profile of v1, /device:TPU:32, one launch (start us, length us, event | category | flops | bytes accessed | tf_op | source)
XLA Modules:
  0.0 31.0 jit_solution(17883504034132859110)
XLA Ops:
  0.7 29.7 %shard_map.64 = bf16[1,2048]{1,0:T(2,128)(2,1)S(1)} custom-call(bf16[1,2048]{1,0:T(2,128)(2,1)} %q_ref.1, bf16[512,1024]{1,0:T(8,128)(2,1)} %k_ref.1, bf16[512,1024]{1,0:T(8,128)(2,1)} %v_ref.1, bf16[1,256,1024]{2,1,0:T(8,128)(2,1)} %sk_ref.1, bf16[1,256,1024]{2,1,0:T(8,128)(2,1)} %sv_ref.1, s32[1]{0:T(128)S(6)} %copy.9.len_ref), custom_call_target="tpu_custom_call" | custom-call | tf_op jit(solution)/shard_map/pallas_call | solution.py:336
  30.4 0.6 %copy.8 = bf16[1,2048]{1,0:T(2,128)(2,1)} copy(bf16[1,2048]{1,0:T(2,128)(2,1)S(1)} %shard_map.64) | data formatting | bytes 8192
